TPU v7x, 32 devices: a whole 2x2x4 slice. The times are simulated.
32 devices in a mesh: parts: 2 (over y), rep: 4 (over x, core), tp: 4 (over z).
Axes of the slice: x: 2, y: 2, z: 4, core: 2. Of those that a mesh axis runs over, the one named last changes fastest.
Arguments:
- tokens: bfloat16 [8192, 5120], P(('parts', 'rep', 'tp')), parts along dimension 0, may hold values from -6 to 6
- q_weight: bfloat16 [5120, 8192], P(None, 'tp'), may hold values from -0.078125 to 0.078125
- a_store: bfloat16 [1024, 5120, 32], P(('parts', 'rep'), 'tp'), parts along dimension 0, may hold values from -0.078125 to 0.078125
- b_store: bfloat16 [1024, 32, 8192], P(('parts', 'rep'), None, 'tp'), parts along dimension 0, may hold values from -1 to 1
- store_row: int32 [1024], P('parts'), parts along dimension 0, may hold values from 0 to 511, as said below
- block_adapter: int32 [8, 8], P('parts'), parts along dimension 0, may hold values from 0 to 511, as said below
- block_length: int32 [8, 8], P('parts'), parts along dimension 0, may hold values from 1 to 128, as said below
Outputs:
- queries: bfloat16 [8192, 8192], P(('parts', 'rep'), 'tp'), parts along dimension 0
There are 2 independent parts, one for each index of `parts`. A program takes and returns all parts, laid end to end along the dimension named above; an argument that names none is the same for every part. Nothing has to cross between parts.
Inputs may be any that keep to these rules, and one draw needn't show every extreme that they name: `store_row`: a permutation of 0 to 511. `block_adapter`: within one replica's 8 blocks, at most 2 blocks name adapters held by the same replica, and in every replica some holder serves exactly 2 of them. `block_length`: every replica has a block with all 128 rows live.
All inputs are finite; a program needn't handle non-finite values.
Results may differ from a plain program's by a relative error of at most 0.004.
Values may be sent and summed in bfloat16 or wider, within the bound.
A program may use at most 192 MiB of HBM per device.

v0:
```python
import jax
import jax.numpy as jnp
from jax import lax
from jax.sharding import PartitionSpec as P


def per_device(tokens, q_weight, a_store, b_store, store_row, block_adapter, block_length):
    replicas = lax.axis_size("rep")
    here_rep = lax.axis_index("rep")
    tp_index = lax.axis_index("tp")
    slot_count = a_store.shape[0]
    width_slice = a_store.shape[1]
    rank_dim = a_store.shape[2]
    out_cols = b_store.shape[2]
    model_width = tokens.shape[1]
    blocks = block_adapter.shape[1]
    capacity = max(2, -(-blocks // replicas))
    local_rows = tokens.shape[0]
    total_rows = local_rows * lax.axis_size("tp")
    block_rows = total_rows // blocks
    stored = jnp.take(store_row, block_adapter, axis=0)
    owner_rep = stored // slot_count
    local_slot = stored % slot_count
    owned = (owner_rep == here_rep).astype(jnp.int32)
    earlier_owned = jnp.cumsum(owned, axis=1) - owned
    places = jnp.arange(capacity, dtype=jnp.int32)
    picked = (owned[:, None, :] == 1) & (earlier_owned[:, None, :] == places[None, :, None])
    pick_int = picked.astype(jnp.int32)
    source_slot = jnp.sum(pick_int * local_slot[:, None, :], axis=2).reshape(-1)
    filled = jnp.sum(pick_int, axis=2).reshape(-1) > 0
    shrink_out = jnp.where(
        filled[:, None, None], jnp.take(a_store, source_slot, axis=0), jnp.zeros((), a_store.dtype)
    )
    expand_out = jnp.where(
        filled[:, None, None], jnp.take(b_store, source_slot, axis=0), jnp.zeros((), b_store.dtype)
    )
    shrink_out = shrink_out.reshape(replicas, capacity, width_slice, rank_dim)
    expand_out = expand_out.reshape(replicas, capacity, rank_dim, out_cols)
    shrink_in, expand_in = (
        lax.all_to_all(shrink_out, "rep", split_axis=0, concat_axis=0, tiled=True),
        lax.all_to_all(expand_out, "rep", split_axis=0, concat_axis=0, tiled=True),
    )
    self_owner = jnp.take(owner_rep, here_rep, axis=0)
    block_ids = jnp.arange(blocks, dtype=jnp.int32)
    earlier_same = (self_owner[None, :] == self_owner[:, None]) & (
        block_ids[None, :] < block_ids[:, None]
    )
    rank_here = jnp.sum(earlier_same.astype(jnp.int32), axis=1)
    recv_index = self_owner * capacity + rank_here
    fetched_a = jnp.take(
        shrink_in.reshape(replicas * capacity, width_slice, rank_dim), recv_index, axis=0
    )
    fetched_b = jnp.take(
        expand_in.reshape(replicas * capacity, rank_dim, out_cols), recv_index, axis=0
    )
    live_counts = jnp.take(block_length, here_rep, axis=0)
    valid_rows = jnp.arange(block_rows, dtype=jnp.int32)[None, :] < live_counts[:, None]
    first_row = tp_index * local_rows
    row_block = (first_row + jnp.arange(local_rows, dtype=jnp.int32)) // block_rows
    all_blocks = jnp.einsum(
        "td,bdr->tbr",
        tokens,
        lax.all_gather(fetched_a, "tp", axis=1, tiled=True),
        preferred_element_type=jnp.float32,
    )
    selector = (row_block[:, None] == block_ids[None, :]).astype(jnp.float32)
    own_low = jnp.einsum("tbr,tb->tr", all_blocks, selector).astype(jnp.bfloat16)
    joined = jnp.concatenate([tokens, own_low], axis=1)
    piece = lax.all_gather(joined, "tp", axis=0, tiled=True)
    base_piece = jnp.dot(piece[:, :model_width], q_weight, preferred_element_type=jnp.float32)
    combined = jnp.concatenate([base_piece, piece[:, model_width:].astype(jnp.float32)], axis=1)
    base_out = combined[:, :out_cols]
    low_rank = combined[:, out_cols:].astype(jnp.bfloat16).reshape(blocks, block_rows, rank_dim)
    adapter_out = jnp.einsum(
        "bnr,brq->bnq", low_rank, fetched_b, preferred_element_type=jnp.float32
    )
    adapter_out = jnp.where(valid_rows[:, :, None], adapter_out, jnp.float32(0.0))
    return (base_out + adapter_out.reshape(total_rows, out_cols)).astype(jnp.bfloat16)


def solution(mesh):
    return jax.shard_map(
        per_device,
        mesh=mesh,
        in_specs=(
            P(("parts", "rep", "tp"), None),
            P(None, "tp"),
            P(("parts", "rep"), "tp", None),
            P(("parts", "rep"), None, "tp"),
            P("parts"),
            P("parts", None),
            P("parts", None),
        ),
        out_specs=P(("parts", "rep"), "tp"),
        check_vma=False,
    )
```

profile of v0, /device:TPU:0, one launch (start us, length us, event | category | flops | bytes accessed | tf_op | source)
XLA Modules:
  0.0 319.2 jit_solution(10147449203117539495)
XLA Ops:
  6.5 0.0 copy-start
  6.5 0.7 compare_select_fusion
  7.2 0.1 reshape.216
  7.3 0.0 copy-done
  7.3 0.7 gather_fusion
  8.0 0.1 reshape.215
  8.1 0.7 add_select_fusion
  8.8 0.7 broadcast_compare_fusion
  9.5 0.2 reduce_window_sum.11
  9.7 0.2 convert_reduce_fusion
  9.9 0.1 copy.12
  10.0 0.1 copy.11
  10.1 0.1 copy.10
  10.2 0.1 reshape.166
  10.3 4.6 %gather_fusion.1 = bf16[8,1280,32]{1,2,0:T(8,128)(2,1)S(1)} fusion(bf16[128,1280,32]{1,2,0:T(8,128)(2,1)} %param.11, s32[1024]{0:T(1024)S(1)} %pad_clamp_fusion.1), kind=kCustom, calls=%fused_computation.1 | custom fusion | bytes 1310752 | tf_op jit(solution)/shard_map/jit(_take)/gather | solution.py:32
  14.9 1.0 select_select_fusion.1
  15.9 4.2 %all-to-all-start = ((bf16[4,2,1280,32]{2,3,1,0:T(8,128)(2,1)}), bf16[4,2,1280,32]{2,3,1,0:T(8,128)(2,1)S(1)}, u32[]{:S(2)}, u32[]{:S(2)}) async-start(bf16[4,2,1280,32]{2,3,1,0:T(8,128)(2,1)} %select_select_fusion.1), calls=%async_computation | async-start | bytes 1310720 | tf_op jit(solution)/shard_map/all_to_all | solution.py:40
  20.1 0.0 all-gather.3.cloned.1.call-start
  20.1 0.2 convert_reduce_fusion.1
  20.3 10.0 %all-to-all-done = bf16[4,2,1280,32]{2,3,1,0:T(8,128)(2,1)S(1)} async-done(((bf16[4,2,1280,32]{2,3,1,0:T(8,128)(2,1)}), bf16[4,2,1280,32]{2,3,1,0:T(8,128)(2,1)S(1)}, u32[]{:S(2)}, u32[]{:S(2)}) %all-to-all-start) | async-done | bytes 655392 | tf_op jit(solution)/shard_map/all_to_all | solution.py:40
  30.3 0.6 gather_fusion.2
  30.9 1.0 broadcast_select_fusion
  31.9 0.0 copy-start.2
  31.9 0.0 all-gather.3.cloned.1.call-update
  31.9 0.0 all-gather.5.cloned.1.call-start
  32.0 0.1 fusion.15
  32.1 55.8 %all-gather.3.cloned.1.call-done = bf16[8,5120,32]{1,2,0:T(8,128)(2,1)} async-done(((bf16[8,1280,32]{1,2,0:T(8,128)(2,1)}), bf16[8,5120,32]{1,2,0:T(8,128)(2,1)}) %all-gather.3.cloned.1.call-update) | async-done | bytes 2621456 | tf_op jit(solution)/shard_map/all_gather | solution.py:63
  87.9 3.4 %fusion.7 = bf16[256,8,32]{0,2,1:T(8,128)(2,1)S(1)} fusion(bf16[8,5120,32]{1,2,0:T(8,128)(2,1)} %all-gather.3.cloned.1.call-done, bf16[256,5120]{1,0:T(8,128)(2,1)} %param.9), kind=kOutput, calls=%fused_computation.13 | convolution fusion | flops 671088640 | bytes 5373952 | tf_op jit(solution)/shard_map/td,bdr->tbr/dot_general | solution.py:60
  91.3 0.3 copy.17
  91.6 0.4 fusion.13
  92.0 0.0 copy-done.2
  92.0 1.7 pad_maximum_fusion
  93.7 0.0 all-gather.5.cloned.1.call-update
  93.8 6.6 %gather_fusion.3 = bf16[8,32,2048]{2,1,0:T(8,128)(2,1)S(1)} fusion(bf16[128,32,2048]{2,1,0:T(8,128)(2,1)} %param.12, s32[1024]{0:T(1024)S(1)} %pad_clamp_fusion.1), kind=kCustom, calls=%fused_computation.3 | custom fusion | bytes 2097184 | tf_op jit(solution)/shard_map/jit(_take)/gather | solution.py:35
  100.4 1.2 select_select_fusion
  101.5 3.5 %all-to-all-start.1 = ((bf16[4,2,32,2048]{3,2,1,0:T(8,128)(2,1)}), bf16[4,2,32,2048]{3,2,1,0:T(8,128)(2,1)S(1)}, u32[]{:S(2)}, u32[]{:S(2)}) async-start(bf16[4,2,32,2048]{3,2,1,0:T(8,128)(2,1)} %select_select_fusion), calls=%async_computation.1 | async-start | bytes 2097152 | tf_op jit(solution)/shard_map/all_to_all | solution.py:41
  105.1 0.7 fusion.20
  105.8 0.1 iota_compare_fusion.1
  105.8 13.7 %all-to-all-done.1 = bf16[4,2,32,2048]{3,2,1,0:T(8,128)(2,1)S(1)} async-done(((bf16[4,2,32,2048]{3,2,1,0:T(8,128)(2,1)}), bf16[4,2,32,2048]{3,2,1,0:T(8,128)(2,1)S(1)}, u32[]{:S(2)}, u32[]{:S(2)}) %all-to-all-start.1) | async-done | bytes 1048608 | tf_op jit(solution)/shard_map/all_to_all | solution.py:41
  119.5 0.6 gather_fusion.4
  120.1 160.8 %all-gather.5.cloned.1.call-done = bf16[1024,5152]{1,0:T(8,128)(2,1)} async-done(((bf16[256,5152]{1,0:T(8,128)(2,1)}), bf16[1024,5152]{1,0:T(8,128)(2,1)}) %all-gather.5.cloned.1.call-update) | async-done | bytes 10551312 | tf_op jit(solution)/shard_map/all_gather | solution.py:69
  280.9 1.0 slice.26
  281.9 1.3 convolution_select_fusion
  283.2 0.0 copy-start.1
  283.2 29.2 %fusion.2 = bf16[1024,2048]{1,0:T(8,128)(2,1)} fusion(f32[8,128,2048]{2,1,0:T(8,128)S(1)} %convolution_select_fusion, bf16[5120,2048]{1,0:T(8,128)(2,1)} %param.10, bf16[1024,5152]{1,0:T(8,128)(2,1)} %all-gather.5.cloned.1.call-done), kind=kOutput, calls=%fused_computation.8 | convolution fusion | flops 21479030784 | bytes 44040192 | tf_op jit(solution)/shard_map/dot_general | solution.py:70
  312.4 0.0 copy-done.1
  (10 shorter events, 0.1 us)
Async XLA Ops:
  6.5 0.8 copy-start
  15.9 14.5 %all-to-all-start = ((bf16[4,2,1280,32]{2,3,1,0:T(8,128)(2,1)}), bf16[4,2,1280,32]{2,3,1,0:T(8,128)(2,1)S(1)}, u32[]{:S(2)}, u32[]{:S(2)}) async-start(bf16[4,2,1280,32]{2,3,1,0:T(8,128)(2,1)} %select_select_fusion.1), calls=%async_computation | async-start | bytes 1310720 | tf_op jit(solution)/shard_map/all_to_all | solution.py:40
  20.1 67.8 %all-gather.3.cloned.1.call-start = ((), (), s32[]{:S(2)}) async-start(), calls=%async_computation.2 | async-start | bytes 3276800 | tf_op jit(solution)/shard_map/all_gather | solution.py:63
  31.9 60.1 %copy-start.2 = (bf16[256,5120]{1,0:T(8,128)(2,1)S(1)}, bf16[256,5120]{1,0:T(8,128)(2,1)}, u32[]{:S(2)}) copy-start(bf16[256,5120]{1,0:T(8,128)(2,1)} %param.9) | copy-start | bytes 7864324
  31.9 249.0 %all-gather.5.cloned.1.call-start = ((), (), s32[]{:S(2)}) async-start(), calls=%async_computation.3 | async-start | bytes 13434880 | tf_op jit(solution)/shard_map/all_gather | solution.py:69
  101.5 18.0 %all-to-all-start.1 = ((bf16[4,2,32,2048]{3,2,1,0:T(8,128)(2,1)}), bf16[4,2,32,2048]{3,2,1,0:T(8,128)(2,1)S(1)}, u32[]{:S(2)}, u32[]{:S(2)}) async-start(bf16[4,2,32,2048]{3,2,1,0:T(8,128)(2,1)} %select_select_fusion), calls=%async_computation.1 | async-start | bytes 2097152 | tf_op jit(solution)/shard_map/all_to_all | solution.py:41
  283.2 29.2 %copy-start.1 = (s32[512]{0:T(512)S(1)}, s32[512]{0:T(512)}, u32[]{:S(2)}) copy-start(s32[512]{0:T(512)} %param.13) | copy-start | bytes 6148
Sparse Core Ops, SparseCore 0:
  32.0 55.7 all-gather.2
  93.9 187.0 all-gather.4
where the time goes:
time: 320 us; the launch traced here: 319 us
  waiting for transfers between devices  240 us (75%)
  matrix products  34.3 us (11%)
  local copies, waits for them, and re-layouts  14.9 us (5%)
  between operations  13.5 us (4%)
  other arithmetic  8.38 us (3%)
  starting transfers between devices  7.79 us (2%)
    all_gather x1, waiting for transfers between devices, per_device(): piece = lax.all_gather(joined, 'tp', axis=0, tiled=True)  161 us
    all_gather x1, waiting for transfers between devices, per_device(): lax.all_gather(fetched_a, 'tp', axis=1, tiled=True)  55.8 us
    dot_general x1, matrix products, per_device(): jnp.dot(piece[:, :model_width], q_weight, preferred_element_type=jnp.floa...  29.2 us
    all_to_all x1, waiting for transfers between devices, per_device(): lax.all_to_all(expand_out, 'rep', split_axis=0, concat_axis=0, tiled=True)  13.7 us
    all_to_all x1, waiting for transfers between devices, per_device(): lax.all_to_all(shrink_out, 'rep', split_axis=0, concat_axis=0, tiled=True)  10 us
    gather x1, local copies, waits for them, and re-layouts, per_device(): jnp.take(b_store, source_slot, axis=0)  6.59 us
  transfers between devices with their start and end apart: 4, of which 4 were waited for; matrix products, arithmetic and copies ran while one was open for 3% of the time, Pallas kernels for 0%

commit v1 on v0

v1 whole, which is shorter than its diff:
```python
import functools

import jax
import jax.numpy as jnp
from jax import lax
from jax.experimental import pallas as pl
from jax.experimental.pallas import tpu as pltpu
from jax.sharding import PartitionSpec as P

MESH = pl.DeviceIdType.MESH


def kernel(
    n, reps, ch, block_rows,
    recv_ref, live_ref, tok_hbm, w_hbm, a_out, b_out, o_hbm,
    w, toks, obuf, a_in, b_in, a_sel, a_own, low,
    w_sem, own_sem, out_sem, rsend, lsend, trecv,
    a_send, a_recv, b_send, b_recv, ta_send, ta_recv, low_send, low_recv,
):
    me = lax.axis_index("tp")
    rep = lax.axis_index("rep")
    rows_own = toks.shape[1]
    chunks = rows_own // ch
    cols = obuf.shape[1]
    blocks, rank, width = a_sel.shape
    per_dev = a_own.shape[1]
    cap = a_out.shape[1]
    tile = min(512, cols)

    barrier = pltpu.get_barrier_semaphore()
    for i in range(1, n):
        pl.semaphore_signal(
            barrier, inc=1, device_id={"tp": lax.rem(me + i, n)}, device_id_type=MESH)
    for i in range(1, reps):
        pl.semaphore_signal(
            barrier, inc=1, device_id={"rep": lax.rem(rep + i, reps)}, device_id_type=MESH)
    pl.semaphore_wait(barrier, n - 1 + reps - 1)

    def chunk_rows(c):
        return pl.ds(pl.multiple_of(c * ch, ch), ch)

    def send(src, s, c, to, sems):
        return pltpu.make_async_remote_copy(
            src_ref=src, dst_ref=toks.at[s, chunk_rows(c)],
            send_sem=sems.at[s, c], recv_sem=trecv.at[s, c],
            device_id={"tp": to}, device_id_type=MESH)

    def right_send(src, s, c):
        return send(src, s, c, jnp.minimum(me + 1, n - 1), rsend)

    def left_send(src, s, c):
        return send(src, s, c, jnp.maximum(me - 1, 0), lsend)

    def send_own(c):
        src = tok_hbm.at[chunk_rows(c)]

        @pl.when(me < n - 1)
        def _():
            right_send(src, me, c).start()

        @pl.when(me > 0)
        def _():
            left_send(src, me, c).start()

    def rep_copy(src, dst, to, sends, recvs):
        return pltpu.make_async_remote_copy(
            src_ref=src.at[to], dst_ref=dst.at[rep],
            send_sem=sends.at[to], recv_sem=recvs.at[rep],
            device_id={"rep": to}, device_id_type=MESH)

    def rep_arrival(dst, frm, sends, recvs):
        return pltpu.make_async_remote_copy(
            src_ref=dst.at[frm], dst_ref=dst.at[frm],
            send_sem=sends.at[frm], recv_sem=recvs.at[frm],
            device_id={"rep": frm}, device_id_type=MESH)

    early = max(1, chunks // 2)
    for i in range(1, reps):
        rep_copy(a_out, a_in, lax.rem(rep + i, reps), a_send, a_recv).start()
    for c in range(early):
        send_own(c)
    own_a = pltpu.make_async_copy(a_out.at[rep], a_in.at[rep], a_recv.at[rep])
    own_b = pltpu.make_async_copy(b_out.at[rep], b_in.at[rep], b_recv.at[rep])
    own_a.start()
    for i in range(1, reps):
        rep_copy(b_out, b_in, lax.rem(rep + i, reps), b_send, b_recv).start()
    own_b.start()
    own_t = pltpu.make_async_copy(tok_hbm, toks.at[me], own_sem)
    own_t.start()
    w_copy = pltpu.make_async_copy(w_hbm, w, w_sem)
    w_copy.start()

    own_a.wait()
    for i in range(1, reps):
        rep_arrival(a_in, lax.rem(rep + i, reps), a_send, a_recv).wait_recv()
    for b in range(blocks):
        at = recv_ref[b]
        a_sel[b] = a_in[at // cap, at % cap]

    def first_block(d):
        return d * rows_own // block_rows

    def ta_copy(d):
        return pltpu.make_async_remote_copy(
            src_ref=a_sel.at[pl.ds(first_block(d), per_dev)], dst_ref=a_own.at[me],
            send_sem=ta_send.at[d], recv_sem=ta_recv.at[me],
            device_id={"tp": d}, device_id_type=MESH)

    def ta_arrival(d):
        return pltpu.make_async_remote_copy(
            src_ref=a_own.at[d], dst_ref=a_own.at[d],
            send_sem=ta_send.at[d], recv_sem=ta_recv.at[d],
            device_id={"tp": d}, device_id_type=MESH)

    for i in range(1, n):
        ta_copy(lax.rem(me + i, n)).start()
    for c in range(early, chunks):
        send_own(c)
    a_own[me] = a_sel[pl.ds(first_block(me), per_dev)]
    own_t.wait()
    for i in range(1, n):
        ta_arrival(lax.rem(me + i, n)).wait_recv()

    part = rows_own // per_dev
    for j in range(per_dev):
        total = jnp.zeros((part, rank), jnp.float32)
        for k in range(n):
            total += lax.dot_general(
                toks[me, j * part:(j + 1) * part, k * width:(k + 1) * width], a_own[k, j],
                (((1,), (1,)), ((), ())), preferred_element_type=jnp.float32)
        low[me, j * part:(j + 1) * part, :] = total.astype(jnp.bfloat16)

    def low_copy(d):
        return pltpu.make_async_remote_copy(
            src_ref=low.at[me], dst_ref=low.at[me],
            send_sem=low_send.at[d], recv_sem=low_recv.at[me],
            device_id={"tp": d}, device_id_type=MESH)

    def low_arrival(d):
        return pltpu.make_async_remote_copy(
            src_ref=low.at[d], dst_ref=low.at[d],
            send_sem=low_send.at[d], recv_sem=low_recv.at[d],
            device_id={"tp": d}, device_id_type=MESH)

    for i in range(1, n):
        low_copy(lax.rem(me + i, n)).start()

    own_b.wait()
    for i in range(1, reps):
        rep_arrival(b_in, lax.rem(rep + i, reps), b_send, b_recv).wait_recv()
    w_copy.wait()

    def out_copy(s, c):
        at = pl.ds(pl.multiple_of(s * rows_own + c * ch, ch), ch)
        return pltpu.make_async_copy(obuf.at[at], o_hbm.at[at], out_sem.at[s, c])

    def multiply(s, c):
        block = (s * rows_own + c * ch) // block_rows
        inside = lax.rem(s * rows_own + c * ch, block_rows)
        at = recv_ref[block]
        live = live_ref[block]
        here = pl.ds(pl.multiple_of(s * rows_own + c * ch, ch), ch)
        valid = inside + lax.broadcasted_iota(jnp.int32, (ch, tile), 0) < live

        @pl.loop(0, cols // tile)
        def _(t):
            cs = pl.ds(pl.multiple_of(t * tile, tile), tile)
            extra = jnp.dot(
                low[s, chunk_rows(c), :], b_in[at // cap, at % cap, :, cs],
                preferred_element_type=jnp.float32)
            base = jnp.dot(
                toks[s, chunk_rows(c), :], w[:, cs], preferred_element_type=jnp.float32)
            obuf[here, cs] = (base + jnp.where(valid, extra, 0.0)).astype(jnp.bfloat16)

        out_copy(s, c).start()

    @pl.loop(0, chunks)
    def _(c):
        multiply(me, c)

    @pl.loop(0, (n - 1) * chunks)
    def _(e):
        k = e // chunks + 1
        c = lax.rem(e, chunks)
        from_left = jnp.maximum(me - k, 0)
        from_right = jnp.minimum(me + k, n - 1)

        @pl.when(me - k >= 0)
        def _():
            here = toks.at[from_left, chunk_rows(c)]
            right_send(here, from_left, c).wait_recv()

            @pl.when(me < n - 1)
            def _():
                right_send(here, from_left, c).start()

        @pl.when(me + k < n)
        def _():
            here = toks.at[from_right, chunk_rows(c)]
            left_send(here, from_right, c).wait_recv()

            @pl.when(me > 0)
            def _():
                left_send(here, from_right, c).start()

        @pl.when(me - k >= 0)
        def _():
            @pl.when(c == 0)
            def _():
                low_arrival(from_left).wait_recv()

            multiply(from_left, c)

        @pl.when(me + k < n)
        def _():
            @pl.when(c == 0)
            def _():
                low_arrival(from_right).wait_recv()

            multiply(from_right, c)

    for i in range(1, reps):
        to = lax.rem(rep + i, reps)
        rep_copy(a_out, a_in, to, a_send, a_recv).wait_send()
        rep_copy(b_out, b_in, to, b_send, b_recv).wait_send()
    for i in range(1, n):
        to = lax.rem(me + i, n)
        ta_copy(to).wait_send()
        low_copy(to).wait_send()

    @pl.loop(0, n * chunks)
    def _(e):
        s = e // chunks
        c = lax.rem(e, chunks)
        here = toks.at[s, chunk_rows(c)]
        out_copy(s, c).wait()

        @pl.when((s <= me) & (me < n - 1))
        def _():
            right_send(here, s, c).wait_send()

        @pl.when((s >= me) & (me > 0))
        def _():
            left_send(here, s, c).wait_send()


def per_device(tokens, q_weight, a_store, b_store, store_row, block_adapter, block_length):
    n = lax.axis_size("tp")
    reps = lax.axis_size("rep")
    here_rep = lax.axis_index("rep")
    slot_count, width, rank = a_store.shape
    cols = b_store.shape[2]
    rows_own, model_width = tokens.shape
    blocks = block_adapter.shape[1]
    cap = max(2, -(-blocks // reps))
    block_rows = rows_own * n // blocks
    ch = min(64, rows_own)
    chunks = rows_own // ch
    per_dev = max(1, rows_own // block_rows)

    stored = jnp.take(store_row, block_adapter, axis=0, mode="clip")
    owner = stored // slot_count
    slot = stored % slot_count
    ids = jnp.arange(blocks, dtype=jnp.int32)
    earlier = (owner[:, :, None] == owner[:, None, :]) & (ids[None, None, :] < ids[None, :, None])
    place = jnp.sum(earlier.astype(jnp.int32), axis=2)
    picked = (owner == here_rep)[:, None, :] & (
        place[:, None, :] == jnp.arange(cap, dtype=jnp.int32)[None, :, None])
    source = jnp.sum(jnp.where(picked, slot[:, None, :], 0), axis=2).reshape(-1)
    a_t = jnp.transpose(a_store, (0, 2, 1))
    a_out = jnp.take(a_t, source, axis=0, mode="clip").reshape(reps, cap, rank, width)
    b_out = jnp.take(b_store, source, axis=0, mode="clip").reshape(reps, cap, rank, cols)
    mine = (jnp.arange(reps, dtype=jnp.int32) == here_rep)[:, None]
    recv = jnp.sum(jnp.where(mine, owner * cap + place, 0), axis=0)
    live = jnp.sum(jnp.where(mine, block_length, 0), axis=0)

    any_spec = pl.BlockSpec(memory_space=pl.ANY)
    smem = pl.BlockSpec(memory_space=pltpu.SMEM)
    dma = pltpu.SemaphoreType.DMA
    bf16 = jnp.bfloat16
    rows = rows_own * n
    return pl.pallas_call(
        functools.partial(kernel, n, reps, ch, block_rows),
        out_shape=jax.ShapeDtypeStruct((rows, cols), bf16),
        in_specs=[smem, smem, any_spec, any_spec, any_spec, any_spec],
        out_specs=any_spec,
        scratch_shapes=[
            pltpu.VMEM((model_width, cols), bf16),
            pltpu.VMEM((n, rows_own, model_width), bf16),
            pltpu.VMEM((rows, cols), bf16),
            pltpu.VMEM((reps, cap, rank, width), bf16),
            pltpu.VMEM((reps, cap, rank, cols), bf16),
            pltpu.VMEM((blocks, rank, width), bf16),
            pltpu.VMEM((n, per_dev, rank, width), bf16),
            pltpu.VMEM((n, rows_own, rank), bf16),
            dma, dma, dma((n, chunks)), dma((n, chunks)), dma((n, chunks)), dma((n, chunks)),
            dma((reps,)), dma((reps,)), dma((reps,)), dma((reps,)),
            dma((n,)), dma((n,)), dma((n,)), dma((n,)),
        ],
        compiler_params=pltpu.CompilerParams(
            collective_id=0, has_side_effects=True, vmem_limit_bytes=50 * 1024 * 1024),
        cost_estimate=pl.CostEstimate(
            flops=2 * rows * model_width * cols, bytes_accessed=2 * model_width * cols,
            transcendentals=0),
    )(recv, live, tokens, q_weight, a_out, b_out)


def solution(mesh):
    return jax.shard_map(
        per_device,
        mesh=mesh,
        in_specs=(
            P(("parts", "rep", "tp"), None),
            P(None, "tp"),
            P(("parts", "rep"), "tp", None),
            P(("parts", "rep"), None, "tp"),
            P("parts"),
            P("parts", None),
            P("parts", None),
        ),
        out_specs=P(("parts", "rep"), "tp"),
        check_vma=False,
    )
```

time: 320 us -> 215 us (0.67)
  waiting for transfers between devices: 240 us -> 0 us
  Pallas kernels: 0 us -> 196 us
  matrix products: 34.3 us -> 0 us
  between operations: 13.5 us -> 0.05 us
  starting transfers between devices: 7.79 us -> 0 us
  other arithmetic: 8.38 us -> 1.19 us
    all_gather x2 -> x0, waiting for transfers between devices: 217 us -> none  [the longest x1 161 us: per_device(): piece = lax.all_gather(joined, 'tp', axis=0, tiled=True)]
    pallas_call x0 -> x1, Pallas kernels: none -> 196 us  [per_device(): pl.pallas_call(functools.partial(kernel, n, reps, ch, block_rows), out_sh...]
    dot_general x4 -> x0, matrix products: 34.3 us -> none  [the longest x1 29.2 us: per_device(): jnp.dot(piece[:, :model_width], q_weight, preferred_element_type=jnp.floa...]
    all_to_all x2 -> x0, waiting for transfers between devices: 23.7 us -> none  [the longest x1 13.7 us: per_device(): lax.all_to_all(expand_out, 'rep', split_axis=0, concat_axis=0, tiled=True)]
    all_to_all x2 -> x0, starting transfers between devices: 7.75 us -> none  [the longest x1 4.21 us: per_device(): lax.all_to_all(shrink_out, 'rep', split_axis=0, concat_axis=0, tiled=True)]
    select_n x9 -> x1, other arithmetic: 5.24 us -> 0.01 us  [per_device(): slot = stored % slot_count]
    unnamed x6 -> x3, local copies, waits for them, and re-layouts: 0.01 us -> 4.79 us
    gather x6 -> x4, local copies, waits for them, and re-layouts: 13.2 us -> 11.7 us  [the longest x1 6.38 us: per_device(): jnp.take(b_store, source, axis=0, mode='clip')]
  transfers between devices with their start and end apart: 4 -> 0, of which waited for: 4 -> 0; matrix products, arithmetic and copies ran while one was open for 3% -> 0% of each run, Pallas kernels for 0% -> 0%
where the time goes in v1:
time: 215 us
  Pallas kernels  196 us (91%)
  local copies, waits for them, and re-layouts  17.5 us (8%)
    pallas_call x1, Pallas kernels, per_device(): pl.pallas_call(functools.partial(kernel, n, reps, ch, block_rows), out_sh...  196 us
    gather x1, local copies, waits for them, and re-layouts, per_device(): jnp.take(b_store, source, axis=0, mode='clip')  6.38 us
    unnamed x3, local copies, waits for them, and re-layouts  4.79 us
    gather x1, local copies, waits for them, and re-layouts, per_device(): jnp.take(a_t, source, axis=0, mode='clip').reshape(reps, cap, rank, width)  4.57 us

profile of v1, /device:TPU:0, one launch (start us, length us, event | category | flops | bytes accessed | tf_op | source)
XLA Modules:
  0.0 214.7 jit_solution(4207537395767029364)
XLA Ops:
  0.0 0.0 copy-start
  0.0 0.8 reshape.82
  0.8 0.0 copy-done
  0.8 0.7 gather_fusion
  1.5 0.1 reshape.81
  1.6 0.2 convert_reduce_fusion
  1.9 0.2 select_reduce_fusion
  2.0 0.8 select_reduce_fusion.1
  2.8 0.1 copy.8
  2.9 0.1 reshape.90
  3.0 4.6 %gather_fusion.1 = bf16[8,32,1280]{2,1,0:T(8,128)(2,1)S(1)} fusion(bf16[128,32,1280]{2,1,0:T(8,128)(2,1)} %bitcast.5, s32[1024]{0:T(1024)S(1)} %pad_clamp_fusion), kind=kCustom, calls=%fused_computation.1 | custom fusion | bytes 1310752 | tf_op jit(solution)/shard_map/jit(_take)/gather | solution.py:271
  7.5 6.4 %gather_fusion.2 = bf16[8,32,2048]{2,1,0:T(8,128)(2,1)S(1)} fusion(bf16[128,32,2048]{2,1,0:T(8,128)(2,1)} %param.10, s32[1024]{0:T(1024)S(1)} %pad_clamp_fusion), kind=kCustom, calls=%fused_computation.2 | custom fusion | bytes 2097184 | tf_op jit(solution)/shard_map/jit(_take)/gather | solution.py:272
  13.9 195.9 %shard_map.73 = bf16[1024,2048]{1,0:T(8,128)(2,1)} custom-call(s32[8]{0:T(128)S(1)} %get-tuple-element.6.recv_ref, s32[8]{0:T(128)S(1)} %get-tuple-element.5.live_ref, bf16[256,5120]{1,0:T(8,128)(2,1)} %tok_hbm.1, bf16[5120,2048]{1,0:T(8,128)(2,1)} %w_hbm.1, bf16[4,2,32,1280]{3,2,1,0:T(8,128)(2,1)S(1)} %bitcast.4, bf16[4,2,32,2048]{3,2,1,0:T(8,128)(2,1)S(1)} %bitcast.3), custom_call_target="tpu_custom_call" | custom-call | flops 21474836480 | bytes 20971520 | tf_op jit(solution)/shard_map/pallas_call | solution.py:282
  209.9 4.8 %copy.10 = bf16[1024,2048]{1,0:T(8,128)(2,1)} copy(bf16[1024,2048]{1,0:T(8,128)(2,1)} %shard_map.73) | data formatting | bytes 8388608
  (6 shorter events, 0.1 us)
Async XLA Ops:
  0.0 0.8 copy-start

commit v2 on v1

--- a/solution.py
+++ b/solution.py
@@ -13,7 +13,7 @@
 def kernel(
     n, reps, ch, block_rows,
     recv_ref, live_ref, tok_hbm, w_hbm, a_out, b_out, o_hbm,
-    w, toks, obuf, a_in, b_in, a_sel, a_own, low,
+    w, toks, obuf, a_in, b_in, a_sel, a_own, low, low_t,
     w_sem, own_sem, out_sem, rsend, lsend, trecv,
     a_send, a_recv, b_send, b_recv, ta_send, ta_recv, low_send, low_recv,
 ):
@@ -129,16 +129,17 @@
                 toks[me, j * part:(j + 1) * part, k * width:(k + 1) * width], a_own[k, j],
                 (((1,), (1,)), ((), ())), preferred_element_type=jnp.float32)
         low[me, j * part:(j + 1) * part, :] = total.astype(jnp.bfloat16)
+        low_t[me, :, j * part:(j + 1) * part] = total.T.astype(jnp.bfloat16)
 
     def low_copy(d):
         return pltpu.make_async_remote_copy(
-            src_ref=low.at[me], dst_ref=low.at[me],
+            src_ref=low_t.at[me], dst_ref=low_t.at[me],
             send_sem=low_send.at[d], recv_sem=low_recv.at[me],
             device_id={"tp": d}, device_id_type=MESH)
 
     def low_arrival(d):
         return pltpu.make_async_remote_copy(
-            src_ref=low.at[d], dst_ref=low.at[d],
+            src_ref=low_t.at[d], dst_ref=low_t.at[d],
             send_sem=low_send.at[d], recv_sem=low_recv.at[d],
             device_id={"tp": d}, device_id_type=MESH)
 
@@ -174,9 +175,9 @@
 
         out_copy(s, c).start()
 
-    @pl.loop(0, chunks)
-    def _(c):
-        multiply(me, c)
+    def take_low(s):
+        low_arrival(s).wait_recv()
+        low[s] = low_t[s].astype(jnp.float32).T.astype(jnp.bfloat16)
 
     @pl.loop(0, (n - 1) * chunks)
     def _(e):
@@ -207,7 +208,7 @@
         def _():
             @pl.when(c == 0)
             def _():
-                low_arrival(from_left).wait_recv()
+                take_low(from_left)
 
             multiply(from_left, c)
 
@@ -215,9 +216,13 @@
         def _():
             @pl.when(c == 0)
             def _():
-                low_arrival(from_right).wait_recv()
+                take_low(from_right)
 
             multiply(from_right, c)
+
+        @pl.when(k == min(2, n - 1))
+        def _():
+            multiply(me, c)
 
     for i in range(1, reps):
         to = lax.rem(rep + i, reps)
@@ -242,6 +247,57 @@
         @pl.when((s >= me) & (me > 0))
         def _():
             left_send(here, s, c).wait_send()
+
+
+def fetch(
+    reps, cap,
+    row_ref, adapter_ref, length_ref, a_hbm, b_hbm, a_out, b_out, recv_ref, live_ref,
+    source, seen, a_sem, b_sem,
+):
+    rep = lax.axis_index("rep")
+    slots = a_hbm.shape[0]
+    blocks = adapter_ref.shape[1]
+    for i in range(reps * cap):
+        source[i] = 0
+    for i in range(reps):
+        seen[i] = 0
+
+    @pl.loop(0, reps)
+    def _(r):
+        def block(b, held):
+            stored = row_ref[adapter_ref[r, b]]
+            mine = stored // slots == rep
+
+            @pl.when(mine)
+            def _():
+                source[r * cap + jnp.minimum(held, cap - 1)] = stored % slots
+
+            return held + mine.astype(jnp.int32)
+
+        lax.fori_loop(0, blocks, block, jnp.int32(0))
+
+    def copies(i):
+        at = source[i]
+        return (
+            pltpu.make_async_copy(a_hbm.at[at], a_out.at[i], a_sem.at[i]),
+            pltpu.make_async_copy(b_hbm.at[at], b_out.at[i], b_sem.at[i]),
+        )
+
+    for i in range(reps * cap):
+        for copy in copies(i):
+            copy.start()
+
+    @pl.loop(0, blocks)
+    def _(b):
+        owner = row_ref[adapter_ref[rep, b]] // slots
+        place = seen[owner]
+        recv_ref[b] = owner * cap + place
+        seen[owner] = place + 1
+        live_ref[b] = length_ref[rep, b]
+
+    for i in range(reps * cap):
+        for copy in copies(i):
+            copy.wait()
 
 
 def per_device(tokens, q_weight, a_store, b_store, store_row, block_adapter, block_length):
@@ -258,27 +314,29 @@
     chunks = rows_own // ch
     per_dev = max(1, rows_own // block_rows)
 
-    stored = jnp.take(store_row, block_adapter, axis=0, mode="clip")
-    owner = stored // slot_count
-    slot = stored % slot_count
-    ids = jnp.arange(blocks, dtype=jnp.int32)
-    earlier = (owner[:, :, None] == owner[:, None, :]) & (ids[None, None, :] < ids[None, :, None])
-    place = jnp.sum(earlier.astype(jnp.int32), axis=2)
-    picked = (owner == here_rep)[:, None, :] & (
-        place[:, None, :] == jnp.arange(cap, dtype=jnp.int32)[None, :, None])
-    source = jnp.sum(jnp.where(picked, slot[:, None, :], 0), axis=2).reshape(-1)
-    a_t = jnp.transpose(a_store, (0, 2, 1))
-    a_out = jnp.take(a_t, source, axis=0, mode="clip").reshape(reps, cap, rank, width)
-    b_out = jnp.take(b_store, source, axis=0, mode="clip").reshape(reps, cap, rank, cols)
-    mine = (jnp.arange(reps, dtype=jnp.int32) == here_rep)[:, None]
-    recv = jnp.sum(jnp.where(mine, owner * cap + place, 0), axis=0)
-    live = jnp.sum(jnp.where(mine, block_length, 0), axis=0)
-
     any_spec = pl.BlockSpec(memory_space=pl.ANY)
     smem = pl.BlockSpec(memory_space=pltpu.SMEM)
     dma = pltpu.SemaphoreType.DMA
     bf16 = jnp.bfloat16
     rows = rows_own * n
+    a_t = jnp.transpose(a_store, (0, 2, 1))
+    a_out, b_out, recv, live = pl.pallas_call(
+        functools.partial(fetch, reps, cap),
+        out_shape=(
+            jax.ShapeDtypeStruct((reps * cap, rank, width), bf16),
+            jax.ShapeDtypeStruct((reps * cap, rank, cols), bf16),
+            jax.ShapeDtypeStruct((blocks,), jnp.int32),
+            jax.ShapeDtypeStruct((blocks,), jnp.int32),
+        ),
+        in_specs=[smem, smem, smem, any_spec, any_spec],
+        out_specs=(any_spec, any_spec, smem, smem),
+        scratch_shapes=[
+            pltpu.SMEM((reps * cap,), jnp.int32), pltpu.SMEM((reps,), jnp.int32),
+            dma((reps * cap,)), dma((reps * cap,)),
+        ],
+    )(store_row, block_adapter, block_length, a_t, b_store)
+    a_out = a_out.reshape(reps, cap, rank, width)
+    b_out = b_out.reshape(reps, cap, rank, cols)
     return pl.pallas_call(
         functools.partial(kernel, n, reps, ch, block_rows),
         out_shape=jax.ShapeDtypeStruct((rows, cols), bf16),
@@ -293,12 +351,13 @@
             pltpu.VMEM((blocks, rank, width), bf16),
             pltpu.VMEM((n, per_dev, rank, width), bf16),
             pltpu.VMEM((n, rows_own, rank), bf16),
+            pltpu.VMEM((n, rank, rows_own), bf16),
             dma, dma, dma((n, chunks)), dma((n, chunks)), dma((n, chunks)), dma((n, chunks)),
             dma((reps,)), dma((reps,)), dma((reps,)), dma((reps,)),
             dma((n,)), dma((n,)), dma((n,)), dma((n,)),
         ],
         compiler_params=pltpu.CompilerParams(
-            collective_id=0, has_side_effects=True, vmem_limit_bytes=50 * 1024 * 1024),
+            collective_id=0, has_side_effects=True, vmem_limit_bytes=44 * 1024 * 1024),
         cost_estimate=pl.CostEstimate(
             flops=2 * rows * model_width * cols, bytes_accessed=2 * model_width * cols,
             transcendentals=0),

time: 215 us -> 253 us (1.18)
  Pallas kernels: 196 us -> 247 us
  local copies, waits for them, and re-layouts: 17.5 us -> 5.56 us
    pallas_call x0 -> x1, Pallas kernels: none -> 54.9 us  [per_device(): pl.pallas_call(functools.partial(fetch, reps, cap), out_shape=(jax.ShapeD...]
    gather x4 -> x0, local copies, waits for them, and re-layouts: 11.7 us -> none  [the longest x1 6.38 us: per_device(): jnp.take(b_store, source, axis=0, mode='clip')]
    pallas_call x1, Pallas kernels: 196 us -> 192 us  [per_device(): pl.pallas_call(functools.partial(kernel, n, reps, ch, block_rows), out_sh...]
    unnamed x3 -> x11, local copies, waits for them, and re-layouts: 4.79 us -> 5.56 us
where the time goes in v2:
time: 253 us
  Pallas kernels  247 us (98%)
  local copies, waits for them, and re-layouts  5.56 us (2%)
    pallas_call x1, Pallas kernels, per_device(): pl.pallas_call(functools.partial(kernel, n, reps, ch, block_rows), out_sh...  192 us
    pallas_call x1, Pallas kernels, per_device(): pl.pallas_call(functools.partial(fetch, reps, cap), out_shape=(jax.ShapeD...  54.9 us
    unnamed x11, local copies, waits for them, and re-layouts  5.56 us

profile of v2, /device:TPU:0, one launch (start us, length us, event | category | flops | bytes accessed | tf_op | source)
XLA Modules:
  0.0 252.6 jit_solution(5730196619949351700)
XLA Ops:
  0.0 0.0 copy-start
  0.0 54.9 %shard_map.73 = (bf16[8,32,1280]{2,1,0:T(8,128)(2,1)}, bf16[8,32,2048]{2,1,0:T(8,128)(2,1)}, s32[8]{0:T(128)}, s32[8]{0:T(128)}) custom-call(s32[512]{0:T(512)} %row_ref.1, s32[4,8]{1,0:T(4,128)} %adapter_ref.1, s32[4,8]{1,0:T(4,128)} %length_ref.1, bf16[128,32,1280]{2,1,0:T(8,128)(2,1)} %bitcast.5, bf16[128,32,2048]{2,1,0:T(8,128)(2,1)} %b_hbm.1), custom_call_target="tpu_custom_call" | custom-call | tf_op jit(solution)/shard_map/pallas_call | solution.py:323
  54.9 0.0 copy-done
  54.9 0.0 copy-start.1
  54.9 1.2 copy-done.1
  56.1 0.0 copy-start.2
  56.1 1.1 copy-done.2
  57.2 0.0 copy-start.3
  57.2 0.7 copy-done.3
  57.9 0.0 copy-start.4
  57.9 0.6 copy-done.4
  58.4 192.1 %shard_map.74 = bf16[1024,2048]{1,0:T(8,128)(2,1)S(1)} custom-call(s32[8]{0:T(128)S(1)} %copy-done.3, s32[8]{0:T(128)S(1)} %copy-done.4, bf16[256,5120]{1,0:T(8,128)(2,1)S(1)} %copy-done, bf16[5120,2048]{1,0:T(8,128)(2,1)} %w_hbm.1, bf16[4,2,32,1280]{3,2,1,0:T(8,128)(2,1)S(1)} %bitcast.4, bf16[4,2,32,2048]{3,2,1,0:T(8,128)(2,1)S(1)} %bitcast.3), custom_call_target="tpu_custom_call" | custom-call | flops 21474836480 | bytes 20971520 | tf_op jit(solution)/shard_map/pallas_call | solution.py:340
  250.5 2.0 copy.9
Async XLA Ops:
  0.0 54.9 %copy-start = (bf16[256,5120]{1,0:T(8,128)(2,1)S(1)}, bf16[256,5120]{1,0:T(8,128)(2,1)}, u32[]{:S(2)}) copy-start(bf16[256,5120]{1,0:T(8,128)(2,1)} %tok_hbm.1) | copy-start | bytes 7864324
  54.9 1.2 copy-start.1
  56.1 1.1 copy-start.2
  57.2 0.7 copy-start.3
  57.9 0.6 copy-start.4

commit v3 on v2

--- a/solution.py
+++ b/solution.py
@@ -11,16 +11,16 @@
 
 
 def kernel(
-    n, reps, ch, block_rows,
+    n, reps, depth, block_rows,
     recv_ref, live_ref, tok_hbm, w_hbm, a_out, b_out, o_hbm,
-    w, toks, obuf, a_in, b_in, a_sel, a_own, low, low_t,
+    w, toks, obuf, acc, a_in, b_in, a_sel, a_own, low, low_t,
     w_sem, own_sem, out_sem, rsend, lsend, trecv,
     a_send, a_recv, b_send, b_recv, ta_send, ta_recv, low_send, low_recv,
 ):
     me = lax.axis_index("tp")
     rep = lax.axis_index("rep")
     rows_own = toks.shape[1]
-    chunks = rows_own // ch
+    chunks = toks.shape[2] // depth
     cols = obuf.shape[1]
     blocks, rank, width = a_sel.shape
     per_dev = a_own.shape[1]
@@ -36,12 +36,12 @@
             barrier, inc=1, device_id={"rep": lax.rem(rep + i, reps)}, device_id_type=MESH)
     pl.semaphore_wait(barrier, n - 1 + reps - 1)
 
-    def chunk_rows(c):
-        return pl.ds(pl.multiple_of(c * ch, ch), ch)
+    def part_of(c):
+        return pl.ds(pl.multiple_of(c * depth, depth), depth)
 
     def send(src, s, c, to, sems):
         return pltpu.make_async_remote_copy(
-            src_ref=src, dst_ref=toks.at[s, chunk_rows(c)],
+            src_ref=src, dst_ref=toks.at[s, :, part_of(c)],
             send_sem=sems.at[s, c], recv_sem=trecv.at[s, c],
             device_id={"tp": to}, device_id_type=MESH)
 
@@ -52,7 +52,7 @@
         return send(src, s, c, jnp.maximum(me - 1, 0), lsend)
 
     def send_own(c):
-        src = tok_hbm.at[chunk_rows(c)]
+        src = tok_hbm.at[:, part_of(c)]
 
         @pl.when(me < n - 1)
         def _():
@@ -151,29 +151,56 @@
         rep_arrival(b_in, lax.rem(rep + i, reps), b_send, b_recv).wait_recv()
     w_copy.wait()
 
-    def out_copy(s, c):
-        at = pl.ds(pl.multiple_of(s * rows_own + c * ch, ch), ch)
-        return pltpu.make_async_copy(obuf.at[at], o_hbm.at[at], out_sem.at[s, c])
-
-    def multiply(s, c):
-        block = (s * rows_own + c * ch) // block_rows
-        inside = lax.rem(s * rows_own + c * ch, block_rows)
-        at = recv_ref[block]
-        live = live_ref[block]
-        here = pl.ds(pl.multiple_of(s * rows_own + c * ch, ch), ch)
-        valid = inside + lax.broadcasted_iota(jnp.int32, (ch, tile), 0) < live
-
+    def out_rows(s):
+        return pl.ds(pl.multiple_of(s * rows_own, rows_own), rows_own)
+
+    def out_copy(s):
+        return pltpu.make_async_copy(obuf.at[out_rows(s)], o_hbm.at[out_rows(s)], out_sem.at[s])
+
+    def tiles(body):
         @pl.loop(0, cols // tile)
         def _(t):
-            cs = pl.ds(pl.multiple_of(t * tile, tile), tile)
-            extra = jnp.dot(
-                low[s, chunk_rows(c), :], b_in[at // cap, at % cap, :, cs],
-                preferred_element_type=jnp.float32)
-            base = jnp.dot(
-                toks[s, chunk_rows(c), :], w[:, cs], preferred_element_type=jnp.float32)
-            obuf[here, cs] = (base + jnp.where(valid, extra, 0.0)).astype(jnp.bfloat16)
-
-        out_copy(s, c).start()
+            body(pl.ds(pl.multiple_of(t * tile, tile), tile))
+
+    def adapter(s, side):
+        for j in range(per_dev):
+            first = s * rows_own + j * part
+            block = first // block_rows
+            at = recv_ref[block]
+            at_row = lax.broadcasted_iota(jnp.int32, (part, tile), 0)
+            valid = lax.rem(first, block_rows) + at_row < live_ref[block]
+
+            def body(cs):
+                extra = jnp.dot(
+                    low[s, j * part:(j + 1) * part, :], b_in[at // cap, at % cap, :, cs],
+                    preferred_element_type=jnp.float32)
+                acc[side, j * part:(j + 1) * part, cs] = jnp.where(valid, extra, 0.0)
+
+            tiles(body)
+
+    def multiply(s, c, side):
+        @pl.when(c == 0)
+        def _():
+            adapter(s, side)
+
+        def product(cs):
+            return acc[side, :, cs] + jnp.dot(
+                toks[s, :, part_of(c)], w[part_of(c), cs], preferred_element_type=jnp.float32)
+
+        @pl.when(c < chunks - 1)
+        def _():
+            def body(cs):
+                acc[side, :, cs] = product(cs)
+
+            tiles(body)
+
+        @pl.when(c == chunks - 1)
+        def _():
+            def body(cs):
+                obuf[out_rows(s), cs] = product(cs).astype(jnp.bfloat16)
+
+            tiles(body)
+            out_copy(s).start()
 
     def take_low(s):
         low_arrival(s).wait_recv()
@@ -188,7 +215,7 @@
 
         @pl.when(me - k >= 0)
         def _():
-            here = toks.at[from_left, chunk_rows(c)]
+            here = toks.at[from_left, :, part_of(c)]
             right_send(here, from_left, c).wait_recv()
 
             @pl.when(me < n - 1)
@@ -197,7 +224,7 @@
 
         @pl.when(me + k < n)
         def _():
-            here = toks.at[from_right, chunk_rows(c)]
+            here = toks.at[from_right, :, part_of(c)]
             left_send(here, from_right, c).wait_recv()
 
             @pl.when(me > 0)
@@ -210,7 +237,7 @@
             def _():
                 take_low(from_left)
 
-            multiply(from_left, c)
+            multiply(from_left, c, 0)
 
         @pl.when(me + k < n)
         def _():
@@ -218,11 +245,11 @@
             def _():
                 take_low(from_right)
 
-            multiply(from_right, c)
+            multiply(from_right, c, 1)
 
         @pl.when(k == min(2, n - 1))
         def _():
-            multiply(me, c)
+            multiply(me, c, 2)
 
     for i in range(1, reps):
         to = lax.rem(rep + i, reps)
@@ -233,12 +260,15 @@
         ta_copy(to).wait_send()
         low_copy(to).wait_send()
 
+    @pl.loop(0, n)
+    def _(s):
+        out_copy(s).wait()
+
     @pl.loop(0, n * chunks)
     def _(e):
         s = e // chunks
         c = lax.rem(e, chunks)
-        here = toks.at[s, chunk_rows(c)]
-        out_copy(s, c).wait()
+        here = toks.at[s, :, part_of(c)]
 
         @pl.when((s <= me) & (me < n - 1))
         def _():
@@ -310,12 +340,13 @@
     blocks = block_adapter.shape[1]
     cap = max(2, -(-blocks // reps))
     block_rows = rows_own * n // blocks
-    ch = min(64, rows_own)
-    chunks = rows_own // ch
+    depth = model_width // 5
+    chunks = model_width // depth
     per_dev = max(1, rows_own // block_rows)
 
     any_spec = pl.BlockSpec(memory_space=pl.ANY)
     smem = pl.BlockSpec(memory_space=pltpu.SMEM)
+    vmem = pl.BlockSpec(memory_space=pltpu.VMEM)
     dma = pltpu.SemaphoreType.DMA
     bf16 = jnp.bfloat16
     rows = rows_own * n
@@ -329,7 +360,7 @@
             jax.ShapeDtypeStruct((blocks,), jnp.int32),
         ),
         in_specs=[smem, smem, smem, any_spec, any_spec],
-        out_specs=(any_spec, any_spec, smem, smem),
+        out_specs=(vmem, vmem, smem, smem),
         scratch_shapes=[
             pltpu.SMEM((reps * cap,), jnp.int32), pltpu.SMEM((reps,), jnp.int32),
             dma((reps * cap,)), dma((reps * cap,)),
@@ -338,7 +369,7 @@
     a_out = a_out.reshape(reps, cap, rank, width)
     b_out = b_out.reshape(reps, cap, rank, cols)
     return pl.pallas_call(
-        functools.partial(kernel, n, reps, ch, block_rows),
+        functools.partial(kernel, n, reps, depth, block_rows),
         out_shape=jax.ShapeDtypeStruct((rows, cols), bf16),
         in_specs=[smem, smem, any_spec, any_spec, any_spec, any_spec],
         out_specs=any_spec,
@@ -346,13 +377,14 @@
             pltpu.VMEM((model_width, cols), bf16),
             pltpu.VMEM((n, rows_own, model_width), bf16),
             pltpu.VMEM((rows, cols), bf16),
+            pltpu.VMEM((3, rows_own, cols), jnp.float32),
             pltpu.VMEM((reps, cap, rank, width), bf16),
             pltpu.VMEM((reps, cap, rank, cols), bf16),
             pltpu.VMEM((blocks, rank, width), bf16),
             pltpu.VMEM((n, per_dev, rank, width), bf16),
             pltpu.VMEM((n, rows_own, rank), bf16),
             pltpu.VMEM((n, rank, rows_own), bf16),
-            dma, dma, dma((n, chunks)), dma((n, chunks)), dma((n, chunks)), dma((n, chunks)),
+            dma, dma, dma((n,)), dma((n, chunks)), dma((n, chunks)), dma((n, chunks)),
             dma((reps,)), dma((reps,)), dma((reps,)), dma((reps,)),
             dma((n,)), dma((n,)), dma((n,)), dma((n,)),
         ],

time: 253 us -> 200 us (0.79)
  Pallas kernels: 247 us -> 194 us
    pallas_call x1, Pallas kernels: 54.9 us -> 4.32 us  [per_device(): pl.pallas_call(functools.partial(fetch, reps, cap), out_shape=(jax.ShapeD...]
where the time goes in v3:
time: 200 us
  Pallas kernels  194 us (97%)
  local copies, waits for them, and re-layouts  5.56 us (3%)
    pallas_call x1, Pallas kernels, per_device(): pl.pallas_call(functools.partial(kernel, n, reps, depth, block_rows), out...  190 us
    unnamed x11, local copies, waits for them, and re-layouts  5.56 us
    pallas_call x1, Pallas kernels, per_device(): pl.pallas_call(functools.partial(fetch, reps, cap), out_shape=(jax.ShapeD...  4.32 us

profile of v3, /device:TPU:0, one launch (start us, length us, event | category | flops | bytes accessed | tf_op | source)
XLA Modules:
  0.0 199.8 jit_solution(9185989380544676322)
XLA Ops:
  0.0 0.0 copy-start
  0.0 4.3 %shard_map.73 = (bf16[8,32,1280]{2,1,0:T(8,128)(2,1)}, bf16[8,32,2048]{2,1,0:T(8,128)(2,1)}, s32[8]{0:T(128)}, s32[8]{0:T(128)}) custom-call(s32[512]{0:T(512)} %row_ref.1, s32[4,8]{1,0:T(4,128)} %adapter_ref.1, s32[4,8]{1,0:T(4,128)} %length_ref.1, bf16[128,32,1280]{2,1,0:T(8,128)(2,1)} %bitcast.5, bf16[128,32,2048]{2,1,0:T(8,128)(2,1)} %b_hbm.1), custom_call_target="tpu_custom_call" | custom-call | tf_op jit(solution)/shard_map/pallas_call | solution.py:354
  4.3 0.0 copy-done
  4.3 0.0 copy-start.1
  4.4 1.2 copy-done.1
  5.6 0.0 copy-start.2
  5.6 1.1 copy-done.2
  6.7 0.0 copy-start.3
  6.7 0.7 copy-done.3
  7.3 0.0 copy-start.4
  7.3 0.6 copy-done.4
  7.9 189.9 %shard_map.74 = bf16[1024,2048]{1,0:T(8,128)(2,1)S(1)} custom-call(s32[8]{0:T(128)S(1)} %copy-done.3, s32[8]{0:T(128)S(1)} %copy-done.4, bf16[256,5120]{1,0:T(8,128)(2,1)S(1)} %copy-done, bf16[5120,2048]{1,0:T(8,128)(2,1)} %w_hbm.1, bf16[4,2,32,1280]{3,2,1,0:T(8,128)(2,1)S(1)} %bitcast.4, bf16[4,2,32,2048]{3,2,1,0:T(8,128)(2,1)S(1)} %bitcast.3), custom_call_target="tpu_custom_call" | custom-call | flops 21474836480 | bytes 20971520 | tf_op jit(solution)/shard_map/pallas_call | solution.py:371
  197.8 2.0 %copy.9 = bf16[1024,2048]{1,0:T(8,128)(2,1)} copy(bf16[1024,2048]{1,0:T(8,128)(2,1)S(1)} %shard_map.74) | data formatting | bytes 8388608
Async XLA Ops:
  0.0 4.3 %copy-start = (bf16[256,5120]{1,0:T(8,128)(2,1)S(1)}, bf16[256,5120]{1,0:T(8,128)(2,1)}, u32[]{:S(2)}) copy-start(bf16[256,5120]{1,0:T(8,128)(2,1)} %tok_hbm.1) | copy-start | bytes 7864324
  4.3 1.2 copy-start.1
  5.6 1.1 copy-start.2
  6.7 0.7 copy-start.3
  7.3 0.6 copy-start.4

commit v4 on v3

--- a/solution.py
+++ b/solution.py
@@ -117,6 +117,32 @@
     for c in range(early, chunks):
         send_own(c)
     a_own[me] = a_sel[pl.ds(first_block(me), per_dev)]
+    def forward(k, c):
+        from_left = jnp.maximum(me - k, 0)
+        from_right = jnp.minimum(me + k, n - 1)
+
+        @pl.when(me - k >= 0)
+        def _():
+            here = toks.at[from_left, :, part_of(c)]
+            right_send(here, from_left, c).wait_recv()
+
+            @pl.when(me < n - 1)
+            def _():
+                right_send(here, from_left, c).start()
+
+        @pl.when(me + k < n)
+        def _():
+            here = toks.at[from_right, :, part_of(c)]
+            left_send(here, from_right, c).wait_recv()
+
+            @pl.when(me > 0)
+            def _():
+                left_send(here, from_right, c).start()
+
+    @pl.loop(0, chunks)
+    def _(c):
+        forward(1, c)
+
     own_t.wait()
     for i in range(1, n):
         ta_arrival(lax.rem(me + i, n)).wait_recv()
@@ -206,50 +232,34 @@
         low_arrival(s).wait_recv()
         low[s] = low_t[s].astype(jnp.float32).T.astype(jnp.bfloat16)
 
-    @pl.loop(0, (n - 1) * chunks)
+    def take(side, k, c, slot):
+        source = jnp.maximum(me - k, 0) if side == 0 else jnp.minimum(me + k, n - 1)
+
+        @pl.when(me - k >= 0 if side == 0 else me + k < n)
+        def _():
+            @pl.when(c == 0)
+            def _():
+                take_low(source)
+
+            multiply(source, c, slot)
+
+    @pl.loop(chunks, (n - 1) * chunks)
     def _(e):
         k = e // chunks + 1
         c = lax.rem(e, chunks)
-        from_left = jnp.maximum(me - k, 0)
-        from_right = jnp.minimum(me + k, n - 1)
-
-        @pl.when(me - k >= 0)
-        def _():
-            here = toks.at[from_left, :, part_of(c)]
-            right_send(here, from_left, c).wait_recv()
-
-            @pl.when(me < n - 1)
-            def _():
-                right_send(here, from_left, c).start()
-
-        @pl.when(me + k < n)
-        def _():
-            here = toks.at[from_right, :, part_of(c)]
-            left_send(here, from_right, c).wait_recv()
-
-            @pl.when(me > 0)
-            def _():
-                left_send(here, from_right, c).start()
-
-        @pl.when(me - k >= 0)
-        def _():
-            @pl.when(c == 0)
-            def _():
-                take_low(from_left)
-
-            multiply(from_left, c, 0)
-
-        @pl.when(me + k < n)
-        def _():
-            @pl.when(c == 0)
-            def _():
-                take_low(from_right)
-
-            multiply(from_right, c, 1)
-
-        @pl.when(k == min(2, n - 1))
+        take(0, k - 1, c, 0)
+        take(1, k - 1, c, 1)
+
+        @pl.when(k == 2)
         def _():
             multiply(me, c, 2)
+
+        forward(k, c)
+
+        @pl.when(k == n - 1)
+        def _():
+            take(0, k, c, 2)
+            take(1, k, c, 2)
 
     for i in range(1, reps):
         to = lax.rem(rep + i, reps)

time: 200 us -> 212 us (1.060)
  Pallas kernels: 194 us -> 206 us
    pallas_call x1, Pallas kernels: 190 us -> 202 us  [per_device(): pl.pallas_call(functools.partial(kernel, n, reps, depth, block_rows), out...]
where the time goes in v4:
time: 212 us
  Pallas kernels  206 us (97%)
  local copies, waits for them, and re-layouts  5.56 us (3%)
    pallas_call x1, Pallas kernels, per_device(): pl.pallas_call(functools.partial(kernel, n, reps, depth, block_rows), out...  202 us
    unnamed x11, local copies, waits for them, and re-layouts  5.56 us
    pallas_call x1, Pallas kernels, per_device(): pl.pallas_call(functools.partial(fetch, reps, cap), out_shape=(jax.ShapeD...  4.32 us

profile of v4, /device:TPU:0, one launch (start us, length us, event | category | flops | bytes accessed | tf_op | source)
XLA Modules:
  0.0 211.6 jit_solution(10577630452418142397)
XLA Ops:
  0.0 0.0 copy-start
  0.0 4.3 %shard_map.73 = (bf16[8,32,1280]{2,1,0:T(8,128)(2,1)}, bf16[8,32,2048]{2,1,0:T(8,128)(2,1)}, s32[8]{0:T(128)}, s32[8]{0:T(128)}) custom-call(s32[512]{0:T(512)} %row_ref.1, s32[4,8]{1,0:T(4,128)} %adapter_ref.1, s32[4,8]{1,0:T(4,128)} %length_ref.1, bf16[128,32,1280]{2,1,0:T(8,128)(2,1)} %bitcast.5, bf16[128,32,2048]{2,1,0:T(8,128)(2,1)} %b_hbm.1), custom_call_target="tpu_custom_call" | custom-call | tf_op jit(solution)/shard_map/pallas_call | solution.py:364
  4.3 0.0 copy-done
  4.3 0.0 copy-start.1
  4.4 1.2 copy-done.1
  5.6 0.0 copy-start.2
  5.6 1.1 copy-done.2
  6.7 0.0 copy-start.3
  6.7 0.7 copy-done.3
  7.3 0.0 copy-start.4
  7.3 0.6 copy-done.4
  7.9 201.7 %shard_map.74 = bf16[1024,2048]{1,0:T(8,128)(2,1)S(1)} custom-call(s32[8]{0:T(128)S(1)} %copy-done.3, s32[8]{0:T(128)S(1)} %copy-done.4, bf16[256,5120]{1,0:T(8,128)(2,1)S(1)} %copy-done, bf16[5120,2048]{1,0:T(8,128)(2,1)} %w_hbm.1, bf16[4,2,32,1280]{3,2,1,0:T(8,128)(2,1)S(1)} %bitcast.4, bf16[4,2,32,2048]{3,2,1,0:T(8,128)(2,1)S(1)} %bitcast.3), custom_call_target="tpu_custom_call" | custom-call | flops 21474836480 | bytes 20971520 | tf_op jit(solution)/shard_map/pallas_call | solution.py:381
  209.6 2.0 copy.9
Async XLA Ops:
  0.0 4.3 %copy-start = (bf16[256,5120]{1,0:T(8,128)(2,1)S(1)}, bf16[256,5120]{1,0:T(8,128)(2,1)}, u32[]{:S(2)}) copy-start(bf16[256,5120]{1,0:T(8,128)(2,1)} %tok_hbm.1) | copy-start | bytes 7864324
  4.3 1.2 copy-start.1
  5.6 1.1 copy-start.2
  6.7 0.7 copy-start.3
  7.3 0.6 copy-start.4

commit v5 on v4

--- a/solution.py
+++ b/solution.py
@@ -247,6 +247,10 @@
     def _(e):
         k = e // chunks + 1
         c = lax.rem(e, chunks)
+        @pl.when(k < n - 1)
+        def _():
+            forward(k, c)
+
         take(0, k - 1, c, 0)
         take(1, k - 1, c, 1)
 
@@ -254,10 +258,9 @@
         def _():
             multiply(me, c, 2)
 
-        forward(k, c)
-
         @pl.when(k == n - 1)
         def _():
+            forward(k, c)
             take(0, k, c, 2)
             take(1, k, c, 2)
 

time: 212 us -> 201 us (0.948)
  Pallas kernels: 206 us -> 195 us
    pallas_call x1, Pallas kernels: 202 us -> 190 us  [per_device(): pl.pallas_call(functools.partial(kernel, n, reps, depth, block_rows), out...]
where the time goes in v5:
time: 201 us; the launch traced here: 200 us
  Pallas kernels  195 us (97%)
  local copies, waits for them, and re-layouts  5.56 us (3%)
    pallas_call x1, Pallas kernels, per_device(): pl.pallas_call(functools.partial(kernel, n, reps, depth, block_rows), out...  190 us
    unnamed x11, local copies, waits for them, and re-layouts  5.56 us
    pallas_call x1, Pallas kernels, per_device(): pl.pallas_call(functools.partial(fetch, reps, cap), out_shape=(jax.ShapeD...  4.32 us

profile of v5, /device:TPU:0, one launch (start us, length us, event | category | flops | bytes accessed | tf_op | source)
XLA Modules:
  0.0 200.4 jit_solution(10446394032867920298)
XLA Ops:
  0.0 0.0 copy-start
  0.0 4.3 %shard_map.73 = (bf16[8,32,1280]{2,1,0:T(8,128)(2,1)}, bf16[8,32,2048]{2,1,0:T(8,128)(2,1)}, s32[8]{0:T(128)}, s32[8]{0:T(128)}) custom-call(s32[512]{0:T(512)} %row_ref.1, s32[4,8]{1,0:T(4,128)} %adapter_ref.1, s32[4,8]{1,0:T(4,128)} %length_ref.1, bf16[128,32,1280]{2,1,0:T(8,128)(2,1)} %bitcast.5, bf16[128,32,2048]{2,1,0:T(8,128)(2,1)} %b_hbm.1), custom_call_target="tpu_custom_call" | custom-call | tf_op jit(solution)/shard_map/pallas_call | solution.py:367
  4.3 0.0 copy-done
  4.3 0.0 copy-start.1
  4.4 1.2 copy-done.1
  5.6 0.0 copy-start.2
  5.6 1.1 copy-done.2
  6.7 0.0 copy-start.3
  6.7 0.7 copy-done.3
  7.3 0.0 copy-start.4
  7.3 0.6 copy-done.4
  7.9 190.4 %shard_map.74 = bf16[1024,2048]{1,0:T(8,128)(2,1)S(1)} custom-call(s32[8]{0:T(128)S(1)} %copy-done.3, s32[8]{0:T(128)S(1)} %copy-done.4, bf16[256,5120]{1,0:T(8,128)(2,1)S(1)} %copy-done, bf16[5120,2048]{1,0:T(8,128)(2,1)} %w_hbm.1, bf16[4,2,32,1280]{3,2,1,0:T(8,128)(2,1)S(1)} %bitcast.4, bf16[4,2,32,2048]{3,2,1,0:T(8,128)(2,1)S(1)} %bitcast.3), custom_call_target="tpu_custom_call" | custom-call | flops 21474836480 | bytes 20971520 | tf_op jit(solution)/shard_map/pallas_call | solution.py:384
  198.3 2.0 %copy.9 = bf16[1024,2048]{1,0:T(8,128)(2,1)} copy(bf16[1024,2048]{1,0:T(8,128)(2,1)S(1)} %shard_map.74) | data formatting | bytes 8388608
Async XLA Ops:
  0.0 4.3 %copy-start = (bf16[256,5120]{1,0:T(8,128)(2,1)S(1)}, bf16[256,5120]{1,0:T(8,128)(2,1)}, u32[]{:S(2)}) copy-start(bf16[256,5120]{1,0:T(8,128)(2,1)} %tok_hbm.1) | copy-start | bytes 7864324
  4.3 1.2 copy-start.1
  5.6 1.1 copy-start.2
  6.7 0.7 copy-start.3
  7.3 0.6 copy-start.4
